TPU v7x, 512 devices: a whole 4x8x8 slice. The times are simulated.
512 devices in a mesh: grp: 16 (over z, core), dev: 32 (over y, x).
Axes of the slice: x: 4, y: 8, z: 8, core: 2. Of those that a mesh axis runs over, the one named last changes fastest.
Arguments:
- queries: bfloat16 [8192, 768], P(('grp', 'dev')), may hold values from -32 to 32
- passages: bfloat16 [1048576, 768], P(('grp', 'dev')), may hold values from -16 to 16
- list_tiles: int32 [512], P(('grp', 'dev')), may hold values from 1 to 16, 5120 in all
- probes: int32 [8192, 32], P(('grp', 'dev')), may hold values from 0 to 511, all different within a row; in each aligned block of 16 rows (0 to 15, 16 to 31, ...) at most 2 rows name the same one
- fb_probe: int32 [8192, 10], P(('grp', 'dev')), may hold values from 0 to 31, all different within a row
- fb_row: int32 [8192, 10], P(('grp', 'dev')), may hold values from 0 to 127
Outputs:
- retrieved: bfloat16 [8192, 768], P(('grp', 'dev'))
- log_total: float32 [8192], P(('grp', 'dev'))
Inputs may be any that keep to these rules, and one draw needn't show every extreme that they name: `probes`: in each aligned block of 16 queries (the queries of one device) no list is probed by more than 2 of them, a bound that some block reaches; the lists of one query are distinct. The live rows of list l are its first 128 * list_tiles[l] rows; the live tiles of all lists add up to 5120, and some list has all 16. `fb_probe`: the 10 positions of one query are distinct.
All inputs are finite; a program needn't handle non-finite values. No bound on the sum of `list_tiles` on one device may be relied on, other than what follows from the above.
Results may differ from a plain program's by a relative error of at most 0.0071.
Values may be sent and summed in bfloat16 or wider, within the bound.
A program may use at most 64 MiB of HBM per device.

v0:
```python
import math

import jax
import jax.numpy as jnp
from jax import lax
from jax.sharding import PartitionSpec as P

TILE = 128


ALPHA_WEIGHT = 1.0
BETA_WEIGHT = 0.75
NEG_FILL = -1e30


def probe_ranks(block_lists):
    flat_lists = block_lists.reshape(-1)
    position = jnp.arange(flat_lists.shape[0], dtype=jnp.int32)
    same_list = flat_lists[:, None] == flat_lists[None, :]
    earlier = position[:, None] > position[None, :]
    counted = jnp.sum(jnp.logical_and(same_list, earlier), axis=1)
    return counted.reshape(block_lists.shape)


def score_dense(vectors, passages, live_rows):
    row_count = vectors.shape[0]
    block_rows = min(512, row_count)
    score_scale = 3.0 / math.sqrt(vectors.shape[1])
    live_mask = jnp.arange(passages.shape[0], dtype=jnp.int32) < live_rows

    def one_block(slot_block):
        scores = jnp.dot(slot_block, passages.T, preferred_element_type=jnp.float32) * score_scale
        scores = jnp.where(live_mask[None, :], scores, NEG_FILL)
        score_peak = jnp.max(scores, axis=1)
        weights = jnp.exp(scores - score_peak[:, None])
        score_mass = jnp.sum(weights, axis=1)
        partial_value = jnp.dot(
            weights.astype(jnp.bfloat16), passages, preferred_element_type=jnp.float32
        )
        return (partial_value, score_peak, score_mass)

    partial_value, score_peak, score_mass = lax.map(
        one_block, vectors.reshape(row_count // block_rows, block_rows, -1)
    )
    return (
        partial_value.reshape(row_count, -1),
        score_peak.reshape(row_count),
        score_mass.reshape(row_count),
    )


def fold_slots(score_peak, score_mass, partial_value, slot_owner, segments):
    is_live = slot_owner >= 0
    segment_index = jnp.maximum(slot_owner, 0)
    live_peaks = jnp.where(is_live, score_peak, NEG_FILL)
    query_peak = jnp.maximum(
        jax.ops.segment_max(live_peaks, segment_index, num_segments=segments), NEG_FILL
    )
    factor = jnp.where(is_live, jnp.exp(live_peaks - jnp.take(query_peak, segment_index)), 0.0)
    query_mass = jax.ops.segment_sum(factor * score_mass, segment_index, num_segments=segments)
    summed = jax.ops.segment_sum(
        factor[:, None] * partial_value, segment_index, num_segments=segments
    )
    return (query_peak, query_mass, summed)


def slot_vectors(rocchio, slot_owner):
    picked = jnp.take(rocchio, jnp.maximum(slot_owner, 0), axis=0)
    return jnp.where((slot_owner >= 0)[:, None], picked, jnp.zeros_like(picked))


def per_device(queries, passages, list_tiles, probes, fb_probe, fb_row):
    groups = lax.axis_size("grp")
    members = lax.axis_size("dev")
    list_count = groups * members
    query_rows, probe_count = probes.shape
    feature_width = queries.shape[1]
    capacity = min(query_rows, 2 * query_rows * probe_count // list_count)
    slot_count = list_count * capacity
    slot_ranks = probe_ranks(probes)
    probe_slot = probes * capacity + slot_ranks
    fb_slot = jnp.take_along_axis(probe_slot, fb_probe, axis=1).reshape(-1)
    request = jnp.full((slot_count,), -1, jnp.int32).at[fb_slot].set(fb_row.reshape(-1))
    asked_rows = lax.all_to_all(
        lax.all_to_all(
            request.reshape(groups, members, capacity),
            "grp",
            split_axis=0,
            concat_axis=0,
            tiled=True,
        ),
        "dev",
        split_axis=1,
        concat_axis=1,
        tiled=True,
    ).reshape(-1)
    found_rows = jnp.take(passages, jnp.maximum(asked_rows, 0), axis=0)
    found_rows = jnp.where((asked_rows >= 0)[:, None], found_rows, jnp.zeros_like(found_rows))
    returned = lax.all_to_all(
        lax.all_to_all(
            found_rows.reshape(groups, members, capacity, feature_width),
            "grp",
            split_axis=0,
            concat_axis=0,
            tiled=True,
        ),
        "dev",
        split_axis=1,
        concat_axis=1,
        tiled=True,
    )
    fb_rows = jnp.take(returned.reshape(slot_count, feature_width), fb_slot, axis=0)
    fb_rows = fb_rows.astype(jnp.float32).reshape(query_rows, -1, feature_width)
    fb_mean = jnp.sum(fb_rows, axis=1) / fb_rows.shape[1]
    rocchio = (ALPHA_WEIGHT * queries.astype(jnp.float32) + BETA_WEIGHT * fb_mean).astype(
        jnp.bfloat16
    )
    live_tiles = list_tiles[0]

    def score_arrived(arrived):
        return score_dense(arrived, passages, live_tiles * TILE)

    item_query = jnp.arange(query_rows * probe_count, dtype=jnp.int32) // probe_count
    slot_owner = jnp.full((slot_count,), -1, jnp.int32).at[probe_slot.reshape(-1)].set(item_query)
    vectors = slot_vectors(rocchio, slot_owner)
    arrived = lax.all_to_all(
        lax.all_to_all(
            vectors.reshape(groups, members, capacity, feature_width),
            "grp",
            split_axis=0,
            concat_axis=0,
            tiled=True,
        ),
        "dev",
        split_axis=1,
        concat_axis=1,
        tiled=True,
    )
    partial_value, score_peak, score_mass = score_arrived(
        arrived.reshape(slot_count, feature_width)
    )
    part_back, peak_back, mass_back = (
        lax.all_to_all(
            lax.all_to_all(
                partial_value.reshape(groups, members, capacity, feature_width),
                "grp",
                split_axis=0,
                concat_axis=0,
                tiled=True,
            ),
            "dev",
            split_axis=1,
            concat_axis=1,
            tiled=True,
        ),
        lax.all_to_all(
            lax.all_to_all(
                score_peak.reshape(groups, members, capacity),
                "grp",
                split_axis=0,
                concat_axis=0,
                tiled=True,
            ),
            "dev",
            split_axis=1,
            concat_axis=1,
            tiled=True,
        ),
        lax.all_to_all(
            lax.all_to_all(
                score_mass.reshape(groups, members, capacity),
                "grp",
                split_axis=0,
                concat_axis=0,
                tiled=True,
            ),
            "dev",
            split_axis=1,
            concat_axis=1,
            tiled=True,
        ),
    )
    query_peak, query_mass, summed = fold_slots(
        peak_back.reshape(-1),
        mass_back.reshape(-1),
        part_back.reshape(slot_count, feature_width),
        slot_owner,
        query_rows,
    )
    retrieved = (summed / query_mass[:, None]).astype(jnp.bfloat16)
    log_total = query_peak + jnp.log(query_mass)
    return (retrieved, log_total)


def solution(mesh):
    return jax.shard_map(
        per_device,
        mesh=mesh,
        in_specs=(
            P(("grp", "dev"), None),
            P(("grp", "dev"), None),
            P(("grp", "dev")),
            P(("grp", "dev"), None),
            P(("grp", "dev"), None),
            P(("grp", "dev"), None),
        ),
        out_specs=(P(("grp", "dev"), None), P(("grp", "dev"))),
        check_vma=False,
    )
```

profile of v0, /device:TPU:6, one launch (start us, length us, event | category | flops | bytes accessed | tf_op | source)
XLA Modules:
  0.0 520.1 jit_solution(3840383943933543812)
XLA Ops:
  0.6 0.8 eq.15
  1.7 0.7 multiply_add_fusion
  3.3 1.6 gather_fusion.3
  5.7 1.1 scatter_custom_fusion.1
  7.1 17.8 %all_to_all.60 = s32[16,32,2]{1,2,0:T(2,128)S(1)} all-to-all(s32[16,32,2]{1,2,0:T(2,128)S(1)} %copy.77), channel_id=1, replica_groups=mesh['grp'=16,'dev'=32] {'grp'}, dimensions={0} | all-to-all | bytes 8192 | tf_op jit(solution)/shard_map/all_to_all | solution.py:85
  25.1 18.1 %all_to_all.61 = s32[16,32,2]{0,2,1:T(2,128)S(1)} all-to-all(s32[16,32,2]{0,2,1:T(2,128)S(1)} %copy.78), channel_id=1, replica_groups=mesh['grp'=16,'dev'=32] {'dev'}, dimensions={1} | all-to-all | bytes 8192 | tf_op jit(solution)/shard_map/all_to_all | solution.py:84
  44.3 0.9 copy.83
  45.4 5.2 %gather_fusion = bf16[1024,768]{1,0:T(8,128)(2,1)} fusion(bf16[2048,768]{1,0:T(8,128)(2,1)S(1)} %copy-done.1, s32[1024]{0:T(1024)S(1)} %broadcast_clamp_fusion.1), kind=kCustom, calls=%fused_computation | custom fusion | bytes 3149824 | tf_op jit(solution)/shard_map/jit(_take)/gather | solution.py:97
  50.6 4.5 gather.28
  55.1 3.8 broadcast_select_fusion.1
  59.0 41.0 %all_to_all.62 = bf16[16,32,2,768]{3,2,1,0:T(2,128)(2,1)S(1)} all-to-all(bf16[16,32,2,768]{3,2,1,0:T(2,128)(2,1)S(1)} %broadcast_select_fusion.1), channel_id=1, replica_groups=mesh['grp'=16,'dev'=32] {'grp'}, dimensions={0} | all-to-all | bytes 3145728 | tf_op jit(solution)/shard_map/all_to_all | solution.py:100
  100.0 2.8 copy.84
  102.8 6.2 %all-to-all-start.3 = ((bf16[16,32,2,768]{3,2,0,1:T(2,128)(2,1)}), bf16[16,32,2,768]{3,2,0,1:T(2,128)(2,1)}, u32[]{:S(2)}, u32[]{:S(2)}) async-start(bf16[16,32,2,768]{3,2,0,1:T(2,128)(2,1)} %copy.84), calls=%async_computation.3 | async-start | bytes 3145728 | tf_op jit(solution)/shard_map/all_to_all | solution.py:99
  109.1 2.6 scatter_custom_fusion
  111.8 0.9 broadcast_in_dim.109
  112.6 0.9 broadcast_in_dim.111
  114.1 34.8 %all-to-all-done.3 = bf16[16,32,2,768]{3,2,0,1:T(2,128)(2,1)} async-done(((bf16[16,32,2,768]{3,2,0,1:T(2,128)(2,1)}), bf16[16,32,2,768]{3,2,0,1:T(2,128)(2,1)}, u32[]{:S(2)}, u32[]{:S(2)}) %all-to-all-start.3) | async-done | bytes 1572896 | tf_op jit(solution)/shard_map/all_to_all | solution.py:99
  149.0 4.0 copy.85
  153.0 4.6 reshape.176
  157.6 3.4 gather_fusion.1
  161.0 1.0 gather.30
  162.3 0.7 add_convert_fusion
  163.1 5.3 %gather_fusion.2 = bf16[1024,768]{1,0:T(8,128)(2,1)} fusion(bf16[16,768]{1,0:T(8,128)(2,1)S(1)} %add_convert_fusion, s32[1024]{0:T(1024)S(1)} %get-tuple-element.83), kind=kCustom, calls=%fused_computation.2 | custom fusion | bytes 3149824 | tf_op jit(solution)/shard_map/jit(_take)/gather | solution.py:68
  168.3 4.5 gather.32
  172.9 3.8 broadcast_select_fusion.3
  176.7 42.3 %all_to_all.63 = bf16[16,32,2,768]{3,2,1,0:T(2,128)(2,1)S(1)} all-to-all(bf16[16,32,2,768]{3,2,1,0:T(2,128)(2,1)S(1)} %broadcast_select_fusion.3), channel_id=1, replica_groups=mesh['grp'=16,'dev'=32] {'grp'}, dimensions={0} | all-to-all | bytes 3145728 | tf_op jit(solution)/shard_map/all_to_all | solution.py:127
  219.0 2.8 copy.86
  221.8 6.3 %all-to-all-start.5 = ((bf16[16,32,2,768]{3,2,0,1:T(2,128)(2,1)}), bf16[16,32,2,768]{3,2,0,1:T(2,128)(2,1)}, u32[]{:S(2)}, u32[]{:S(2)}) async-start(bf16[16,32,2,768]{3,2,0,1:T(2,128)(2,1)} %copy.86), calls=%async_computation.5 | async-start | bytes 3145728 | tf_op jit(solution)/shard_map/all_to_all | solution.py:126
  228.8 38.9 %all-to-all-done.5 = bf16[16,32,2,768]{3,2,0,1:T(2,128)(2,1)} async-done(((bf16[16,32,2,768]{3,2,0,1:T(2,128)(2,1)}), bf16[16,32,2,768]{3,2,0,1:T(2,128)(2,1)}, u32[]{:S(2)}, u32[]{:S(2)}) %all-to-all-start.5) | async-done | bytes 1572896 | tf_op jit(solution)/shard_map/all_to_all | solution.py:126
  267.6 4.0 copy.87
  271.6 4.7 reshape_reshape.12
  276.3 23.1 %while.15 = (s32[]{:T(128)}, f32[2,512,768]{2,1,0:T(8,128)}, f32[2,512]{1,0:T(2,128)S(1)}, f32[2,512]{1,0:T(2,128)S(1)}, bf16[2,512,768]{2,1,0:T(8,128)(2,1)}, /...) while((s32[]{:T(128)}, f32[2,512,768]{2,1,0:T(8,128)}, ...), condition=%wide.region_7.8_spmd.clone, body=%wide.region_4.7_spmd.clone.sunk | while | flops 3232760832 | bytes 38036612 | solution.py:42
  276.3 3.1 fusion.50
  279.5 1.9 copy-done
  281.4 0.9 fusion.51
  282.4 5.5 %bitcast_dynamic-update-slice_fusion.2 = f32[2,512,768]{2,1,0:T(8,128)} fusion(f32[2,512,768]{2,1,0:T(8,128)} %get-tuple-element.158, s32[]{:T(128)} %get-tuple-element.157, bf16[2048,768]{1,0:T(8,128)(2,1)S(1)} %get-tuple-element.171, f32[512,2048]{1,0:T(8,128)} %copy-done, f32[512]{0:T(512)S(1)} %get-tuple-element.147, ...), kind=kOutput, calls=%fused_computation.20.clone.1 | convolution fusion | flops 1614807040 | bytes 8917504 | tf_op jit(solution)/shard_map/while/body/eval_jaxpr/dot_general | solution.py:37
  287.9 3.1 fusion.50
  291.1 1.9 copy-done
  293.0 0.9 fusion.51
  294.0 5.5 %bitcast_dynamic-update-slice_fusion.2 = f32[2,512,768]{2,1,0:T(8,128)} fusion(f32[2,512,768]{2,1,0:T(8,128)} %get-tuple-element.158, s32[]{:T(128)} %get-tuple-element.157, bf16[2048,768]{1,0:T(8,128)(2,1)S(1)} %get-tuple-element.171, f32[512,2048]{1,0:T(8,128)} %copy-done, f32[512]{0:T(512)S(1)} %get-tuple-element.147, ...), kind=kOutput, calls=%fused_computation.20.clone.1 | convolution fusion | flops 1614807040 | bytes 8917504 | tf_op jit(solution)/shard_map/while/body/eval_jaxpr/dot_general | solution.py:37
  299.7 0.8 copy.88
  300.5 4.1 all-to-all-start.6
  304.8 0.8 copy.93
  305.6 6.7 %all-to-all-done.6 = f32[16,32,2]{1,2,0:T(2,128)S(1)} async-done(((f32[16,32,2]{1,2,0:T(2,128)}), f32[16,32,2]{1,2,0:T(2,128)S(1)}, u32[]{:S(2)}, u32[]{:S(2)}) %all-to-all-start.6) | async-done | bytes 4128 | tf_op jit(solution)/shard_map/all_to_all | solution.py:157
  312.2 3.4 all-to-all-start.10
  316.3 6.9 %all-to-all-done.10 = f32[16,32,2]{1,2,0:T(2,128)S(1)} async-done(((f32[16,32,2]{1,2,0:T(2,128)}), f32[16,32,2]{1,2,0:T(2,128)S(1)}, u32[]{:S(2)}, u32[]{:S(2)}) %all-to-all-start.10) | async-done | bytes 4128 | tf_op jit(solution)/shard_map/all_to_all | solution.py:170
  323.2 5.6 %all-to-all-start.7 = ((f32[16,32,2]{0,2,1:T(2,128)}), f32[16,32,2]{0,2,1:T(2,128)S(1)}, u32[]{:S(2)}, u32[]{:S(2)}) async-start(f32[16,32,2]{0,2,1:T(2,128)} %copy.89), calls=%async_computation.7 | async-start | bytes 65536 | tf_op jit(solution)/shard_map/all_to_all | solution.py:156
  328.8 5.2 reshape_reshape.14
  333.9 3.0 all-to-all-done.7
  336.9 3.7 all-to-all-start.8
  341.4 71.0 %all-to-all-done.8 = f32[16,32,2,768]{3,2,1,0:T(2,128)S(1)} async-done(((f32[16,32,2,768]{3,2,1,0:T(2,128)}), f32[16,32,2,768]{3,2,1,0:T(2,128)S(1)}, u32[]{:S(2)}, u32[]{:S(2)}) %all-to-all-start.8) | async-done | bytes 3145760 | tf_op jit(solution)/shard_map/all_to_all | solution.py:144
  412.4 6.8 %all-to-all-start.11 = ((f32[16,32,2]{0,2,1:T(2,128)}), f32[16,32,2]{0,2,1:T(2,128)S(1)}, u32[]{:S(2)}, u32[]{:S(2)}) async-start(f32[16,32,2]{0,2,1:T(2,128)} %copy.94), calls=%async_computation.11 | async-start | bytes 65536 | tf_op jit(solution)/shard_map/all_to_all | solution.py:169
  419.2 3.4 copy.91
  422.6 4.8 all-to-all-done.11
  427.3 5.9 %all-to-all-start.9 = ((f32[16,32,2,768]{3,2,0,1:T(2,128)}), f32[16,32,2,768]{3,2,0,1:T(2,128)S(1)}, u32[]{:S(2)}, u32[]{:S(2)}) async-start(f32[16,32,2,768]{3,2,0,1:T(2,128)} %copy.91), calls=%async_computation.9 | async-start | bytes 6291456 | tf_op jit(solution)/shard_map/all_to_all | solution.py:143
  434.3 7.7 %scatter_custom_fusion.2 = f32[16]{0:T(128)S(1)} fusion(s32[1024]{0:T(1024)} %get-tuple-element.84, f32[1024]{0:T(1024)S(1)} %broadcast_select_fusion.4, f32[]{:T(128)} %constant.138.clone.1), kind=kCustom, calls=%fused_computation.88 | custom fusion | flops 1024 | bytes 576 | tf_op jit(solution)/shard_map/scatter-max | solution.py:57
  442.1 0.7 fusion.39
  442.8 9.9 %fusion.27 = f32[1024]{0:T(1024)S(1)} fusion(f32[1024]{0:T(1024)S(1)} %reshape.179, pred[1024]{0:T(1024)(128)(4,1)S(1)} %get-tuple-element.82, f32[]{:T(128)} %bitcast.4, f32[]{:T(128)} %bitcast.5, f32[]{:T(128)} %bitcast.6, f32[]{:T(128)} %bitcast.7, f32[]{:T(128)} %bitcast.8, f32[]{:T(128)} %bitcast.9, f32[]{:T(128)} %bitcast.10, f32[1024]{0:T(1024)S(1)} %reshape.177, ...), kind=kLoop, calls=%fused_computation.58 | loop fusion | flops 37888 | bytes 17472 | tf_op jit(solution)/shard_map/mul | solution.py:60
  452.7 7.7 %scatter_custom_fusion.4 = f32[16]{0:T(128)S(1)} fusion(s32[1024]{0:T(1024)} %get-tuple-element.84, f32[1024]{0:T(1024)S(1)} %fusion.27, f32[]{:T(128)} %constant.93.clone.1), kind=kCustom, calls=%fused_computation.85 | custom fusion | flops 1024 | bytes 576 | tf_op jit(solution)/shard_map/scatter-add | solution.py:60
  461.0 9.9 %fusion.26 = f32[1024]{0:T(1024)S(1)} fusion(pred[1024]{0:T(1024)(128)(4,1)S(1)} %get-tuple-element.82, f32[]{:T(128)} %bitcast.4, f32[]{:T(128)} %bitcast.5, f32[]{:T(128)} %bitcast.6, f32[]{:T(128)} %bitcast.7, f32[]{:T(128)} %bitcast.8, f32[]{:T(128)} %bitcast.9, f32[]{:T(128)} %bitcast.10, f32[1024]{0:T(1024)S(1)} %reshape.177, f32[]{:T(128)} %bitcast.19, ...), kind=kLoop, calls=%fused_computation.57 | loop fusion | flops 36864 | bytes 13376 | tf_op jit(solution)/shard_map/jit(_where)/select_n | solution.py:59
  470.9 33.0 %all-to-all-done.9 = f32[16,32,2,768]{3,2,0,1:T(2,128)S(1)} async-done(((f32[16,32,2,768]{3,2,0,1:T(2,128)}), f32[16,32,2,768]{3,2,0,1:T(2,128)S(1)}, u32[]{:S(2)}, u32[]{:S(2)}) %all-to-all-start.9) | async-done | bytes 3145760 | tf_op jit(solution)/shard_map/all_to_all | solution.py:143
  503.9 3.3 copy.92
  507.2 3.9 reshape.178
  511.1 7.8 %scatter_custom_fusion.3 = f32[16,768]{1,0:T(8,128)S(1)} fusion(s32[1024]{0:T(1024)} %get-tuple-element.84, f32[1024,768]{1,0:T(8,128)S(1)} %reshape.178, f32[1024]{0:T(1024)S(1)} %fusion.26, f32[]{:T(128)} %constant.93.clone.1), kind=kCustom, calls=%fused_computation.28 | custom fusion | flops 1572864 | bytes 3199488 | tf_op jit(solution)/shard_map/scatter-add | solution.py:61
  (63 shorter events, 8.8 us)
Async XLA Ops:
  3.2 1.7 copy-start.4
  3.2 1.9 copy-start.5
  3.3 42.2 %copy-start.1 = (bf16[2048,768]{1,0:T(8,128)(2,1)S(1)}, bf16[2048,768]{1,0:T(8,128)(2,1)}, u32[]{:S(2)}) copy-start(bf16[2048,768]{1,0:T(8,128)(2,1)} %param.9) | copy-start | bytes 9437188
  5.1 0.6 copy-start.6
  100.0 13.5 %copy-start.7 = (s32[160,1]{0,1:T(1,128)S(1)}, s32[160,1]{0,1:T(1,128)}, u32[]{:S(2)}) copy-start(s32[160,1]{0,1:T(1,128)} %copy-done.6) | copy-start | bytes 1924
  102.8 46.1 %all-to-all-start.3 = ((bf16[16,32,2,768]{3,2,0,1:T(2,128)(2,1)}), bf16[16,32,2,768]{3,2,0,1:T(2,128)(2,1)}, u32[]{:S(2)}, u32[]{:S(2)}) async-start(bf16[16,32,2,768]{3,2,0,1:T(2,128)(2,1)} %copy.84), calls=%async_computation.3 | async-start | bytes 3145728 | tf_op jit(solution)/shard_map/all_to_all | solution.py:99
  168.3 4.5 copy-start.2
  168.3 4.5 copy-start.3
  221.8 45.8 %all-to-all-start.5 = ((bf16[16,32,2,768]{3,2,0,1:T(2,128)(2,1)}), bf16[16,32,2,768]{3,2,0,1:T(2,128)(2,1)}, u32[]{:S(2)}, u32[]{:S(2)}) async-start(bf16[16,32,2,768]{3,2,0,1:T(2,128)(2,1)} %copy.86), calls=%async_computation.5 | async-start | bytes 3145728 | tf_op jit(solution)/shard_map/all_to_all | solution.py:126
  279.5 1.9 copy-start
  291.0 1.9 copy-start
  300.5 11.8 %all-to-all-start.6 = ((f32[16,32,2]{1,2,0:T(2,128)}), f32[16,32,2]{1,2,0:T(2,128)S(1)}, u32[]{:S(2)}, u32[]{:S(2)}) async-start(f32[16,32,2]{1,2,0:T(2,128)} %copy.88), calls=%async_computation.6 | async-start | bytes 32768 | tf_op jit(solution)/shard_map/all_to_all | solution.py:157
  312.2 11.0 %all-to-all-start.10 = ((f32[16,32,2]{1,2,0:T(2,128)}), f32[16,32,2]{1,2,0:T(2,128)S(1)}, u32[]{:S(2)}, u32[]{:S(2)}) async-start(f32[16,32,2]{1,2,0:T(2,128)} %copy.93), calls=%async_computation.10 | async-start | bytes 32768 | tf_op jit(solution)/shard_map/all_to_all | solution.py:170
  323.2 13.7 %all-to-all-start.7 = ((f32[16,32,2]{0,2,1:T(2,128)}), f32[16,32,2]{0,2,1:T(2,128)S(1)}, u32[]{:S(2)}, u32[]{:S(2)}) async-start(f32[16,32,2]{0,2,1:T(2,128)} %copy.89), calls=%async_computation.7 | async-start | bytes 65536 | tf_op jit(solution)/shard_map/all_to_all | solution.py:156
  336.9 75.5 %all-to-all-start.8 = ((f32[16,32,2,768]{3,2,1,0:T(2,128)}), f32[16,32,2,768]{3,2,1,0:T(2,128)S(1)}, u32[]{:S(2)}, u32[]{:S(2)}) async-start(f32[16,32,2,768]{3,2,1,0:T(2,128)} %reshape_reshape.14), calls=%async_computation.8 | async-start | bytes 6291456 | tf_op jit(solution)/shard_map/all_to_all | solution.py:144
  412.4 14.9 %all-to-all-start.11 = ((f32[16,32,2]{0,2,1:T(2,128)}), f32[16,32,2]{0,2,1:T(2,128)S(1)}, u32[]{:S(2)}, u32[]{:S(2)}) async-start(f32[16,32,2]{0,2,1:T(2,128)} %copy.94), calls=%async_computation.11 | async-start | bytes 65536 | tf_op jit(solution)/shard_map/all_to_all | solution.py:169
  427.3 76.6 %all-to-all-start.9 = ((f32[16,32,2,768]{3,2,0,1:T(2,128)}), f32[16,32,2,768]{3,2,0,1:T(2,128)S(1)}, u32[]{:S(2)}, u32[]{:S(2)}) async-start(f32[16,32,2,768]{3,2,0,1:T(2,128)} %copy.91), calls=%async_computation.9 | async-start | bytes 6291456 | tf_op jit(solution)/shard_map/all_to_all | solution.py:143
where the time goes:
time: 529 us; the launch traced here: 520 us
  waiting for transfers between devices  199 us (38%)
  blocking collectives  119 us (22%)
  local copies, waits for them, and re-layouts  82.7 us (16%)
  other arithmetic  57.8 us (11%)
  starting transfers between devices  42.1 us (8%)
  matrix products  17.2 us (3%)
    all_to_all x1, waiting for transfers between devices, per_device(): lax.all_to_all(partial_value.reshape(groups, members, capacity, feature_w...  71 us
    all_to_all x1, blocking collectives, per_device(): lax.all_to_all(vectors.reshape(groups, members, capacity, feature_width),...  42.3 us
    all_to_all x1, blocking collectives, per_device(): lax.all_to_all(found_rows.reshape(groups, members, capacity, feature_widt...  41 us
    all_to_all x1, waiting for transfers between devices, per_device(): lax.all_to_all(lax.all_to_all(vectors.reshape(groups, members, capacity,...  38.9 us
    all_to_all x1, waiting for transfers between devices, per_device(): lax.all_to_all(lax.all_to_all(found_rows.reshape(groups, members, capacit...  34.8 us
    all_to_all x1, waiting for transfers between devices, per_device(): lax.all_to_all(lax.all_to_all(partial_value.reshape(groups, members, capa...  33 us
    all_to_all x1, blocking collectives, per_device(): lax.all_to_all(lax.all_to_all(request.reshape(groups, members, capacity),...  18.1 us
    all_to_all x1, blocking collectives, per_device(): lax.all_to_all(request.reshape(groups, members, capacity), 'grp', split_a...  17.8 us
  transfers between devices with their start and end apart: 8, of which 8 were waited for; matrix products, arithmetic and copies ran while one was open for 10% of the time, Pallas kernels for 0%

commit v1 on v0

v1 whole, which is shorter than its diff:
```python
import functools
import math

import jax
import jax.numpy as jnp
from jax import lax
from jax.experimental import pallas as pl
from jax.experimental.pallas import tpu as pltpu
from jax.sharding import PartitionSpec as P

TILE = 128
SLOTS = 2
CORES = 2
LANES = 128
ALPHA_WEIGHT = 1.0
BETA_WEIGHT = 0.75
NEG_FILL = -1e30
F32 = jnp.float32
BF16 = jnp.bfloat16
MESH = pl.DeviceIdType.MESH


def iota(shape, dim):
    return lax.broadcasted_iota(jnp.int32, shape, dim)


def kernel(
    sizes,
    queries_ref,
    probes_ref,
    fb_probe_ref,
    fb_row_ref,
    tiles_ref,
    passages_ref,
    retrieved_ref,
    log_ref,
    held,
    table,
    table_in,
    asked,
    asked_in,
    owner_row,
    select,
    found,
    found_in,
    fsum,
    fsum_in,
    roc,
    roc_in,
    vec,
    vec_in,
    part,
    part_in,
    lse,
    lse_in,
    comb,
    comb_in,
    lse2,
    lse2_in,
    held_sem,
    send_sem,
    recv_sem,
    vec_sem,
):
    groups, members, rows, queries, probe_count, fb_count, width = sizes
    ring = groups // CORES
    across = members // ring
    lists = groups * members
    half = width // 2
    blocks = groups
    slab = SLOTS * blocks
    plane = members
    chunk = ring * slab
    held_queries = blocks * queries
    slots = plane * slab
    tile_lanes = min(LANES, slots)
    per_tile = tile_lanes // slab

    grp, dev = lax.axis_index("grp"), lax.axis_index("dev")
    z, c = grp // CORES, grp % CORES
    y, x = dev // across, dev % across
    my_b = (grp, y * CORES + c)
    my_o = (y, z)
    my_k = (x * ring + y, x * ring + z)

    def outer_id(r, b):
        if r == 0:
            return (b, dev)
        return (z * CORES + b % CORES, (b // CORES) * across + x)

    def plane_id(r, k):
        far_x, far_o = k // ring, k % ring
        if r == 0:
            return (grp, far_o * across + far_x)
        return (far_o * CORES + c, y * across + far_x)

    def to_outer(r, phase, source, target):
        pltpu.make_async_copy(source(my_b[r]), target.at[r, my_b[r]], recv_sem.at[r, phase]).start()

        @pl.loop(1, blocks)
        def _(i):
            b = (my_b[r] + i) % blocks
            pltpu.make_async_remote_copy(
                src_ref=source(b),
                dst_ref=target.at[r, my_b[r]],
                send_sem=send_sem.at[r, phase],
                recv_sem=recv_sem.at[r, phase],
                device_id=outer_id(r, b),
                device_id_type=MESH,
            ).start()

    def to_plane(r, phase, source, target):
        mine = my_k[r]
        pltpu.make_async_copy(source.at[r, mine], target.at[r, mine], recv_sem.at[r, phase]).start()

        @pl.loop(1, plane)
        def _(i):
            k = (mine + i) % plane
            pltpu.make_async_remote_copy(
                src_ref=source.at[r, k],
                dst_ref=target.at[r, mine],
                send_sem=send_sem.at[r, phase],
                recv_sem=recv_sem.at[r, phase],
                device_id=plane_id(r, k),
                device_id_type=MESH,
            ).start()

    def arrived(r, phase, target):
        pltpu.make_async_copy(target.at[r], target.at[r], recv_sem.at[r, phase]).wait()

    def sent(r, phase, target):
        gone = target.at[r, pl.ds(1, target.shape[1] - 1)]
        pltpu.make_async_copy(gone, gone, send_sem.at[r, phase]).wait()

    copy_held = pltpu.make_async_copy(passages_ref, held, held_sem)
    copy_held.start()

    probes = probes_ref[...]
    fb_probe, fb_row = fb_probe_ref[...], fb_row_ref[...]
    position = iota((queries, probe_count), 1)
    wanted = jnp.ones((queries, probe_count), jnp.int32)
    for k in range(fb_count):
        wanted = jnp.where(position == fb_probe[:, k : k + 1], fb_row[:, k : k + 1] + 2, wanted)
    list_lane = iota((queries, lists), 1)
    named = jnp.zeros((queries, lists), jnp.int32)
    for j in range(probe_count):
        named = jnp.where(list_lane == probes[:, j : j + 1], wanted[:, j : j + 1], named)
    member = named > 0
    before = jnp.where(iota((queries, queries), 0) > iota((queries, queries), 1), 1.0, 0.0)
    rank = jnp.dot(
        before.astype(BF16),
        jnp.where(member, 1.0, 0.0).astype(BF16),
        preferred_element_type=F32,
    )
    code = (iota((queries, lists), 0) + 1) * 256 + named
    code = jnp.where(member, code, 0)
    for s in range(SLOTS):
        row = jnp.sum(jnp.where(rank == float(s), code, 0), axis=0, keepdims=True)
        table[0:1, s * lists : (s + 1) * lists] = row
    for r in range(2):
        to_outer(r, 0, lambda b: table, table_in)

    sub_b = iota((blocks, SLOTS * lists), 0)
    lane_l = iota((blocks, lists), 1)
    block_of = iota((slab, 1), 0) % blocks
    turn = iota((slab, LANES), 0) == iota((slab, LANES), 1) % slab
    query_lane = iota((slab, held_queries), 1)
    for r in range(2):
        arrived(r, 0, table_in)
        all_codes = jnp.zeros((blocks, SLOTS * lists), jnp.int32)
        for b in range(blocks):
            all_codes = jnp.where(sub_b == b, table_in[r, b], all_codes)

        @pl.loop(0, plane)
        def _(k, all_codes=all_codes, r=r):
            far_grp, far_dev = plane_id(r, k)
            here = lane_l == far_grp * members + far_dev
            columns = [
                jnp.sum(
                    jnp.where(here, all_codes[:, s * lists : (s + 1) * lists], 0),
                    axis=1,
                    keepdims=True,
                )
                for s in range(SLOTS)
            ]
            column = jnp.concatenate(columns, axis=0)
            owner = column >> 8
            want = (column & 255) - 2
            index = jnp.where(owner > 0, block_of * queries + owner - 1, -1)
            select[r, k] = jnp.where(query_lane == index, 1.0, 0.0).astype(BF16)
            asked[r, k] = jnp.sum(jnp.where(turn, want, 0), axis=0, keepdims=True)
            owner_row[r, k] = jnp.sum(jnp.where(turn, index, 0), axis=0, keepdims=True)

        to_plane(r, 1, asked, asked_in)

    tile_source = iota((1, tile_lanes), 1) // slab
    copy_held.wait()

    def lane_tile(ref, r, j):
        row = ref[r, per_tile * j][:, :tile_lanes]
        for i in range(1, per_tile):
            row = jnp.where(tile_source == i, ref[r, per_tile * j + i][:, :tile_lanes], row)
        return row

    for r in range(2):
        arrived(r, 1, asked_in)
        first = held[0:TILE, r * half : (r + 1) * half]
        for j in range(plane // per_tile):
            row = lane_tile(asked_in, r, j)
            hot = jnp.where(iota((TILE, tile_lanes), 0) == row, 1.0, 0.0).astype(BF16)
            picked = lax.dot_general(
                hot, first, (((0,), (0,)), ((), ())), preferred_element_type=F32
            ).astype(BF16)
            found[r, per_tile * j : per_tile * (j + 1)] = picked.reshape(per_tile, slab, half)
        to_plane(r, 2, found, found_in)

    for r in range(2):
        arrived(r, 2, found_in)
        total = lax.dot_general(
            select[r].reshape(slots, held_queries),
            found_in[r].reshape(slots, half),
            (((0,), (0,)), ((), ())),
            preferred_element_type=F32,
        )
        fsum[r] = total.astype(BF16).reshape(blocks, queries, half)
        to_outer(r, 3, lambda b, r=r: fsum.at[r, b], fsum_in)

    for r in range(2):
        arrived(r, 3, fsum_in)
        total = jnp.zeros((queries, half), F32)
        for b in range(blocks):
            total = total + fsum_in[r, b].astype(F32)
        own = queries_ref[:, r * half : (r + 1) * half].astype(F32)
        roc[r] = (ALPHA_WEIGHT * own + BETA_WEIGHT * (total / fb_count)).astype(BF16)
        to_outer(r, 4, lambda b, r=r: roc.at[r], roc_in)

    for r in range(2):
        arrived(r, 4, roc_in)

    @pl.loop(0, across)
    def _(t):
        far_x = (x + across - t) % across
        for r in range(2):
            vectors = roc_in[r].reshape(held_queries, half)
            there = pl.ds(far_x * ring, ring)
            picked = jnp.dot(
                select[r, there].reshape(chunk, held_queries),
                vectors,
                preferred_element_type=F32,
            )
            vec[r, there] = picked.astype(BF16).reshape(ring, slab, half)

            @pl.when(t == 0)
            def _():
                pltpu.make_async_copy(
                    vec.at[r, my_k[r]], vec_in.at[r, my_k[r]], vec_sem.at[r, x]
                ).start()

            @pl.loop(0, ring)
            def _(i):
                k = far_x * ring + (my_o[r] + i) % ring

                @pl.when(t + i > 0)
                def _():
                    pltpu.make_async_remote_copy(
                        src_ref=vec.at[r, k],
                        dst_ref=vec_in.at[r, my_k[r]],
                        send_sem=send_sem.at[r, 5],
                        recv_sem=vec_sem.at[r, x],
                        device_id=plane_id(r, k),
                        device_id_type=MESH,
                    ).start()

    scale = 3.0 / math.sqrt(width)
    live = tiles_ref[0] * TILE
    bits = slab // 2

    def swapped(index):
        o, s, low = index // slab, (index % slab) // bits, index % bits
        return (low // CORES) * slab + s * bits + o * CORES + low % CORES

    swap = jnp.where(
        iota((chunk, chunk), 0) == swapped(iota((chunk, chunk), 1)), 1.0, 0.0
    ).astype(BF16)

    @pl.loop(0, across)
    def _(t):
        far_x = (x + t) % across
        there = pl.ds(far_x * ring, ring)
        for r in range(2):
            landed = vec_in.at[r, there]
            pltpu.make_async_copy(landed, landed, vec_sem.at[r, far_x]).wait()
        first = vec_in[0, there].reshape(chunk, half)
        second = jnp.dot(
            swap, vec_in[1, there].reshape(chunk, half), preferred_element_type=F32
        ).astype(BF16)
        contract = (((1,), (1,)), ((), ()))
        scores = lax.dot_general(first, held[:, :half], contract, preferred_element_type=F32)
        scores = scores + lax.dot_general(
            second, held[:, half:], contract, preferred_element_type=F32
        )
        scores = jnp.where(iota((chunk, rows), 1) < live, scores * scale, NEG_FILL)
        peak = jnp.max(scores, axis=1, keepdims=True)
        weights = jnp.exp(scores - peak)
        mass = jnp.sum(weights, axis=1, keepdims=True)
        value = jnp.dot(weights.astype(BF16), held[...], preferred_element_type=F32)
        value = (value / mass).astype(BF16)
        level = peak + jnp.log(mass)
        part[0, there] = value[:, :half].reshape(ring, slab, half)
        part[1, there] = (
            jnp.dot(swap, value[:, half:], preferred_element_type=F32)
            .astype(BF16)
            .reshape(ring, slab, half)
        )
        sub, lane = iota((chunk, LANES), 0), iota((chunk, LANES), 1) % slab
        for o in range(ring):
            for r in range(2):
                place = o * slab + lane
                if r == 1:
                    place = swapped(place)
                row = jnp.sum(jnp.where(sub == place, level, 0.0), axis=0, keepdims=True)
                lse[r, far_x * ring + o] = row
        for r in range(2):

            @pl.when(t == 0)
            def _():
                for source, target, phase in ((lse, lse_in, 7), (part, part_in, 6)):
                    pltpu.make_async_copy(
                        source.at[r, my_k[r]], target.at[r, my_k[r]], recv_sem.at[r, phase]
                    ).start()

            @pl.loop(0, ring)
            def _(i):
                k = far_x * ring + (my_o[r] + i) % ring

                @pl.when(t + i > 0)
                def _():
                    for source, target, phase in ((lse, lse_in, 7), (part, part_in, 6)):
                        pltpu.make_async_remote_copy(
                            src_ref=source.at[r, k],
                            dst_ref=target.at[r, my_k[r]],
                            send_sem=send_sem.at[r, phase],
                            recv_sem=recv_sem.at[r, phase],
                            device_id=plane_id(r, k),
                            device_id_type=MESH,
                        ).start()

    sub_q = iota((held_queries, tile_lanes), 0)
    for r in range(2):
        arrived(r, 7, lse_in)
        levels, masks = [], []
        for j in range(plane // per_tile):
            masks.append(sub_q == lane_tile(owner_row, r, j))
            levels.append(jnp.where(masks[-1], lane_tile(lse_in, r, j), NEG_FILL))
        levels = jnp.concatenate(levels, axis=1)
        mask = jnp.concatenate([jnp.where(m, 1.0, 0.0) for m in masks], axis=1)
        top = jnp.max(levels, axis=1, keepdims=True)
        weights = jnp.exp(levels - top) * mask
        total = jnp.sum(weights, axis=1, keepdims=True)
        high = weights.astype(BF16)
        low = (weights - high.astype(F32)).astype(BF16)
        arrived(r, 6, part_in)
        parts = part_in[r].reshape(slots, half)
        value = jnp.dot(high, parts, preferred_element_type=F32)
        value = value + jnp.dot(low, parts, preferred_element_type=F32)
        some = total > 0.0
        total = jnp.where(some, total, 1.0)
        comb[r] = (value / total).astype(BF16).reshape(blocks, queries, half)
        level = jnp.where(some, top + jnp.log(total), NEG_FILL)
        sub, lane = iota((held_queries, LANES), 0), iota((held_queries, LANES), 1) % queries
        for b in range(blocks):
            lse2[r, b] = jnp.sum(
                jnp.where(sub == b * queries + lane, level, 0.0), axis=0, keepdims=True
            )
        to_outer(r, 9, lambda b, r=r: lse2.at[r, b], lse2_in)
        to_outer(r, 8, lambda b, r=r: comb.at[r, b], comb_in)

    square = iota((queries, LANES), 0) == iota((queries, LANES), 1)
    for r in range(2):
        arrived(r, 9, lse2_in)
        level = [
            jnp.sum(jnp.where(square, lse2_in[r, b], 0.0), axis=1, keepdims=True)
            for b in range(blocks)
        ]
        top = functools.reduce(jnp.maximum, level)
        factor = [jnp.exp(v - top) for v in level]
        total = functools.reduce(jnp.add, factor)
        arrived(r, 8, comb_in)
        value = jnp.zeros((queries, half), F32)
        for b in range(blocks):
            value = value + factor[b] * comb_in[r, b].astype(F32)
        retrieved_ref[:, r * half : (r + 1) * half] = (value / total).astype(BF16)
        if r == 0:
            log_total = top + jnp.log(total)
            log_row = jnp.sum(jnp.where(square, log_total, 0.0), axis=0, keepdims=True)
            log_ref[...] = log_row[:, :queries]

    for r in range(2):
        for phase, target in (
            (0, table_in),
            (1, asked_in),
            (2, found_in),
            (3, fsum_in),
            (4, roc_in),
            (5, vec_in),
            (6, part_in),
            (7, lse_in),
            (8, comb_in),
            (9, lse2_in),
        ):
            sent(r, phase, target)


def per_device(queries, passages, list_tiles, probes, fb_probe, fb_row):
    groups, members = lax.axis_size("grp"), lax.axis_size("dev")
    rows, width = passages.shape
    query_rows, probe_count = probes.shape
    fb_count = fb_row.shape[1]
    sizes = (groups, members, rows, query_rows, probe_count, fb_count, width)
    lists, half, slab = groups * members, width // 2, SLOTS * groups
    across = members // (groups // CORES)
    vmem = pl.BlockSpec(memory_space=pltpu.VMEM)
    plane_rows = pltpu.VMEM((2, members, slab, half), BF16)
    plane_int = pltpu.VMEM((2, members, 1, LANES), jnp.int32)
    plane_float = pltpu.VMEM((2, members, 1, LANES), F32)
    outer_rows = pltpu.VMEM((2, groups, query_rows, half), BF16)
    outer_float = pltpu.VMEM((2, groups, 1, LANES), F32)
    retrieved, log_total = pl.pallas_call(
        functools.partial(kernel, sizes),
        out_shape=(
            jax.ShapeDtypeStruct((query_rows, width), BF16),
            jax.ShapeDtypeStruct((1, query_rows), F32),
        ),
        in_specs=[
            vmem,
            vmem,
            vmem,
            vmem,
            pl.BlockSpec(memory_space=pltpu.SMEM),
            pl.BlockSpec(memory_space=pl.ANY),
        ],
        out_specs=(vmem, vmem),
        scratch_shapes=[
            pltpu.VMEM((rows, width), BF16),
            pltpu.VMEM((1, SLOTS * lists), jnp.int32),
            pltpu.VMEM((2, groups, 1, SLOTS * lists), jnp.int32),
            plane_int,
            plane_int,
            plane_int,
            pltpu.VMEM((2, members, slab, groups * query_rows), BF16),
            plane_rows,
            plane_rows,
            outer_rows,
            outer_rows,
            pltpu.VMEM((2, query_rows, half), BF16),
            outer_rows,
            plane_rows,
            plane_rows,
            plane_rows,
            plane_rows,
            plane_float,
            plane_float,
            outer_rows,
            outer_rows,
            outer_float,
            outer_float,
            pltpu.SemaphoreType.DMA,
            pltpu.SemaphoreType.DMA((2, 10)),
            pltpu.SemaphoreType.DMA((2, 10)),
            pltpu.SemaphoreType.DMA((2, across)),
        ],
        compiler_params=pltpu.CompilerParams(
            has_side_effects=True, vmem_limit_bytes=56 * 1024 * 1024
        ),
        name="probe_lists",
    )(queries, probes, fb_probe, fb_row, list_tiles, passages)
    return retrieved, log_total.reshape(query_rows)


def solution(mesh):
    spec = P(("grp", "dev"), None)
    flat = P(("grp", "dev"))
    return jax.shard_map(
        per_device,
        mesh=mesh,
        in_specs=(spec, spec, flat, spec, spec, spec),
        out_specs=(spec, flat),
        check_vma=False,
    )
```

time: 529 us -> 149 us (0.28); the launches traced: 520 us -> 149 us
  waiting for transfers between devices: 199 us -> 0 us
  Pallas kernels: 0 us -> 145 us
  blocking collectives: 119 us -> 0 us
  local copies, waits for them, and re-layouts: 82.7 us -> 2.52 us
  other arithmetic: 57.8 us -> 0 us
  starting transfers between devices: 42.1 us -> 0 us
  matrix products: 17.2 us -> 0 us
    all_to_all x8 -> x0, waiting for transfers between devices: 199 us -> none  [the longest x1 71 us: per_device(): lax.all_to_all(partial_value.reshape(groups, members, capacity, feature_w...]
    pallas_call x0 -> x1, Pallas kernels: none -> 145 us  [per_device(): pl.pallas_call(functools.partial(kernel, sizes), out_shape=(jax.ShapeDtyp...]
    all_to_all x4 -> x0, blocking collectives: 119 us -> none  [the longest x1 42.3 us: per_device(): lax.all_to_all(vectors.reshape(groups, members, capacity, feature_width),...]
    all_to_all x8 -> x0, starting transfers between devices: 42.1 us -> none  [the longest x1 6.79 us: per_device(): lax.all_to_all(lax.all_to_all(score_mass.reshape(groups, members, capacit...]
    gather x10 -> x0, local copies, waits for them, and re-layouts: 26.4 us -> none  [the longest x2 9.81 us: slot_vectors(): picked = jnp.take(rocchio, jnp.maximum(slot_owner, 0), axis=0)]
    all_to_all x12 -> x0, local copies, waits for them, and re-layouts: 22.6 us -> none  [the longest x1 4.02 us: per_device(): lax.all_to_all(lax.all_to_all(vectors.reshape(groups, members, capacity,...]
    select_n x7 -> x0, other arithmetic: 17.5 us -> none  [the longest x1 9.91 us: fold_slots(): jnp.where(is_live, jnp.exp(live_peaks - jnp.take(query_peak, segment_inde...]
    dot_general x4 -> x0, matrix products: 17.2 us -> none  [the longest x2 10.9 us: one_block(): jnp.dot(weights.astype(jnp.bfloat16), passages, preferred_element_type=jn...]
  transfers between devices with their start and end apart: 8 -> 0, of which waited for: 8 -> 0; matrix products, arithmetic and copies ran while one was open for 10% -> 0% of each run, Pallas kernels for 0% -> 0%
where the time goes in v1:
time: 149 us
  Pallas kernels  145 us (97%)
  local copies, waits for them, and re-layouts  2.52 us (2%)
    pallas_call x1, Pallas kernels, per_device(): pl.pallas_call(functools.partial(kernel, sizes), out_shape=(jax.ShapeDtyp...  145 us

profile of v1, /device:TPU:6, one launch (start us, length us, event | category | flops | bytes accessed | tf_op | source)
XLA Modules:
  0.0 148.8 jit_solution(16017469661323198747)
XLA Ops:
  1.3 145.0 %probe_lists.1 = (bf16[16,768]{1,0:T(8,128)(2,1)}, f32[1,16]{1,0:T(1,128)}) custom-call(bf16[16,768]{1,0:T(8,128)(2,1)} %queries_ref.1, s32[16,32]{1,0:T(8,128)} %probes_ref.1, s32[16,10]{1,0:T(8,128)} %fb_probe_ref.1, s32[16,10]{1,0:T(8,128)} %fb_row_ref.1, s32[1]{0:T(128)S(6)} %copy.10.tiles_ref, bf16[2048,768]{1,0:T(8,128)(2,1)} %passages_ref.1), custom_call_target="tpu_custom_call" | custom-call | tf_op jit(solution)/shard_map/probe_lists/pallas_call | solution.py:428
  146.3 1.3 copy.11
  147.6 1.2 copy.12

commit v2 on v1

v2 whole, which is shorter than its diff:
```python
import functools
import math

import jax
import jax.numpy as jnp
from jax import lax
from jax.experimental import pallas as pl
from jax.experimental.pallas import tpu as pltpu
from jax.sharding import PartitionSpec as P

TILE = 128
SLOTS = 2
CORES = 2
LANES = 128
ALPHA_WEIGHT = 1.0
BETA_WEIGHT = 0.75
NEG_FILL = -1e30
F32 = jnp.float32
BF16 = jnp.bfloat16
MESH = pl.DeviceIdType.MESH


def iota(shape, dim):
    return lax.broadcasted_iota(jnp.int32, shape, dim)


def kernel(
    sizes,
    queries_ref,
    probes_ref,
    fb_probe_ref,
    fb_row_ref,
    tiles_ref,
    passages_ref,
    retrieved_ref,
    log_ref,
    held,
    table,
    table_in,
    asked,
    asked_in,
    select,
    spread,
    found,
    found_in,
    fsum,
    fsum_in,
    roc,
    roc_in,
    vec,
    vec_in,
    part,
    part_in,
    lse,
    lse_in,
    comb,
    comb_in,
    lse2,
    lse2_in,
    held_sem,
    send_sem,
    recv_sem,
    vec_sem,
):
    groups, members, rows, queries, probe_count, fb_count, width = sizes
    ring = groups // CORES
    across = members // ring
    lists = groups * members
    half = width // 2
    blocks = groups
    slab = SLOTS * blocks
    plane = members
    chunk = ring * slab
    held_queries = blocks * queries
    slots = plane * slab
    tile_lanes = min(LANES, slots)
    per_tile = tile_lanes // slab

    grp, dev = lax.axis_index("grp"), lax.axis_index("dev")
    z, c = grp // CORES, grp % CORES
    y, x = dev // across, dev % across
    my_b = (grp, y * CORES + c)
    my_o = (y, z)
    my_k = (x * ring + y, x * ring + z)

    def outer_id(r, b):
        if r == 0:
            return (b, dev)
        return (z * CORES + b % CORES, (b // CORES) * across + x)

    def plane_id(r, k):
        far_x, far_o = k // ring, k % ring
        if r == 0:
            return (grp, far_o * across + far_x)
        return (far_o * CORES + c, y * across + far_x)

    def either_way(i, n):
        return jnp.where(i % 2 == 1, (i + 1) // 2, (n - i // 2) % n)

    def send(r, source, target, phase, landed, place):
        pltpu.make_async_remote_copy(
            src_ref=source,
            dst_ref=target,
            send_sem=send_sem.at[r, phase],
            recv_sem=landed,
            device_id=place,
            device_id_type=MESH,
        ).start()

    def to_outer(*items):
        for r in range(2):
            for phase, source, target in items:
                pltpu.make_async_copy(
                    source(r, my_b[r]), target.at[r, my_b[r]], recv_sem.at[r, phase]
                ).start()

        @pl.loop(0, blocks - 1)
        def _(i):
            j = blocks - 1 - i
            step = either_way(j // CORES, ring)
            for r in range(2):
                first = (z, y)[r]
                b = (first + step) % ring * CORES + (c + j) % CORES
                for phase, source, target in items:
                    send(
                        r,
                        source(r, b),
                        target.at[r, my_b[r]],
                        phase,
                        recv_sem.at[r, phase],
                        outer_id(r, b),
                    )

    def to_plane(phase, source, target):
        for r in range(2):
            mine = my_k[r]
            pltpu.make_async_copy(
                source.at[r, mine], target.at[r, mine], recv_sem.at[r, phase]
            ).start()

        @pl.loop(0, plane - 1)
        def _(i):
            j = plane - 1 - i
            step = either_way(j // across, ring)
            for r in range(2):
                k = (x + j) % across * ring + (my_o[r] + step) % ring
                send(
                    r,
                    source.at[r, k],
                    target.at[r, my_k[r]],
                    phase,
                    recv_sem.at[r, phase],
                    plane_id(r, k),
                )

    def to_chunk(t, far_x, *items):
        @pl.when(t == across - 1)
        def _():
            for r in range(2):
                for phase, source, target, landed in items:
                    pltpu.make_async_copy(
                        source.at[r, my_k[r]], target.at[r, my_k[r]], landed(r)
                    ).start()

        @pl.loop(0, ring)
        def _(i):
            step = either_way(ring - 1 - i, ring)

            @pl.when(t + i < across + ring - 2)
            def _():
                for r in range(2):
                    k = far_x * ring + (my_o[r] + step) % ring
                    for phase, source, target, landed in items:
                        send(
                            r,
                            source.at[r, k],
                            target.at[r, my_k[r]],
                            phase,
                            landed(r),
                            plane_id(r, k),
                        )

    def turn_of(t):
        return (across // 2 + either_way(t, across)) % across

    def arrived(r, phase, target):
        pltpu.make_async_copy(target.at[r], target.at[r], recv_sem.at[r, phase]).wait()

    def sent(r, phase, target):
        gone = target.at[r, pl.ds(1, target.shape[1] - 1)]
        pltpu.make_async_copy(gone, gone, send_sem.at[r, phase]).wait()

    barrier = pltpu.get_barrier_semaphore()
    for r in range(2):
        for partners, mine, place in ((blocks, my_b[r], outer_id), (plane, my_k[r], plane_id)):

            @pl.loop(1, partners)
            def _(i, r=r, partners=partners, mine=mine, place=place):
                pl.semaphore_signal(
                    barrier,
                    inc=1,
                    device_id=place(r, (mine + i) % partners),
                    device_id_type=MESH,
                )

    copy_held = pltpu.make_async_copy(passages_ref, held, held_sem)
    copy_held.start()

    probes = probes_ref[...]
    fb_probe, fb_row = fb_probe_ref[...], fb_row_ref[...]
    position = iota((queries, probe_count), 1)
    wanted = jnp.ones((queries, probe_count), jnp.int32)
    for k in range(fb_count):
        wanted = jnp.where(position == fb_probe[:, k : k + 1], fb_row[:, k : k + 1] + 2, wanted)
    list_lane = iota((queries, lists), 1)
    named = jnp.zeros((queries, lists), jnp.int32)
    for j in range(probe_count):
        named = jnp.where(list_lane == probes[:, j : j + 1], wanted[:, j : j + 1], named)
    member = named > 0
    before = jnp.where(iota((queries, queries), 0) > iota((queries, queries), 1), 1.0, 0.0)
    rank = jnp.dot(
        before.astype(BF16),
        jnp.where(member, 1.0, 0.0).astype(BF16),
        preferred_element_type=F32,
    )
    code = (iota((queries, lists), 0) + 1) * 256 + named
    code = jnp.where(member, code, 0)
    for s in range(SLOTS):
        row = jnp.sum(jnp.where(rank == float(s), code, 0), axis=0, keepdims=True)
        table[0:1, s * lists : (s + 1) * lists] = row
    pl.semaphore_wait(barrier, 2 * (blocks - 1 + plane - 1))
    to_outer((0, lambda r, b: table, table_in))

    tiles = plane // per_tile
    list_of = [per_tile * (p % tiles) + p // tiles for p in range(plane)]
    sub_b = iota((blocks, SLOTS * lists), 0)
    sub_p, lane_l = iota((plane, lists), 0), iota((plane, lists), 1)
    far_k = per_tile * (sub_p % tiles) + sub_p // tiles
    lane_slab = iota((tiles, LANES), 1)
    contract_last = (((1,), (1,)), ((), ()))
    slot_codes, list_hots = [], []
    for r in range(2):
        arrived(r, 0, table_in)
        all_codes = jnp.zeros((blocks, SLOTS * lists), jnp.int32)
        for b in range(blocks):
            all_codes = jnp.where(sub_b == b, table_in[r, b], all_codes)
        all_codes = jnp.concatenate(
            [all_codes[:, s * lists : (s + 1) * lists] for s in range(SLOTS)], axis=0
        )
        far_grp, far_dev = plane_id(r, far_k)
        list_hot = jnp.where(lane_l == far_grp * members + far_dev, 1.0, 0.0).astype(BF16)
        want = (all_codes & 255).astype(F32).astype(BF16)
        want_rows = lax.dot_general(
            list_hot,
            jnp.concatenate([want] * (LANES // slab), axis=0),
            contract_last,
            preferred_element_type=F32,
        )
        for p, k in enumerate(list_of):
            asked[r, k] = want_rows[p : p + 1]
        slot_codes.append((all_codes >> 8).astype(F32).astype(BF16))
        list_hots.append(list_hot)
    to_plane(1, asked, asked_in)

    first_of = (iota((slab, plane), 0) % blocks * queries).astype(F32)
    query_lane = iota((slab, held_queries), 1).astype(F32)
    sub_q = iota((held_queries, tile_lanes), 0).astype(F32)
    for r in range(2):
        column = lax.dot_general(
            slot_codes[r], list_hots[r], contract_last, preferred_element_type=F32
        )
        column = jnp.where(column > 0.0, first_of + column - 1.0, -1.0)
        for p, k in enumerate(list_of):
            select[r, k] = jnp.where(query_lane == column[:, p : p + 1], 1.0, 0.0).astype(BF16)
        rows_of = lax.dot_general(
            list_hots[r],
            jnp.concatenate([slot_codes[r]] * (LANES // slab), axis=0),
            contract_last,
            preferred_element_type=F32,
        )
        joined = rows_of[:tiles]
        for i in range(1, per_tile):
            joined = jnp.where(
                lane_slab // slab == i, rows_of[i * tiles : (i + 1) * tiles], joined
            )
        joined = jnp.where(
            joined > 0.0, (lane_slab % blocks * queries).astype(F32) + joined - 1.0, -1.0
        )
        for j in range(tiles):
            spread[r, :, j * tile_lanes : (j + 1) * tile_lanes] = jnp.where(
                sub_q == joined[j : j + 1, :tile_lanes], 1.0, 0.0
            ).astype(BF16)

    tile_source = iota((1, tile_lanes), 1) // slab
    copy_held.wait()

    def lane_tile(ref, r, j):
        row = ref[r, per_tile * j][:, :tile_lanes]
        for i in range(1, per_tile):
            row = jnp.where(tile_source == i, ref[r, per_tile * j + i][:, :tile_lanes], row)
        return row

    for r in range(2):
        arrived(r, 1, asked_in)
        first = held[0:TILE, r * half : (r + 1) * half]
        sub_row = (iota((TILE, tile_lanes), 0) + 2).astype(F32)
        for j in range(tiles):
            row = lane_tile(asked_in, r, j)
            hot = jnp.where(sub_row == row, 1.0, 0.0).astype(BF16)
            picked = lax.dot_general(
                hot, first, (((0,), (0,)), ((), ())), preferred_element_type=F32
            ).astype(BF16)
            found[r, per_tile * j : per_tile * (j + 1)] = picked.reshape(per_tile, slab, half)
    to_plane(2, found, found_in)

    for r in range(2):
        arrived(r, 2, found_in)
        total = jnp.dot(spread[r], found_in[r].reshape(slots, half), preferred_element_type=F32)
        fsum[r] = total.astype(BF16).reshape(blocks, queries, half)
    to_outer((3, lambda r, b: fsum.at[r, b], fsum_in))

    for r in range(2):
        arrived(r, 3, fsum_in)
        total = jnp.zeros((queries, half), F32)
        for b in range(blocks):
            total = total + fsum_in[r, b].astype(F32)
        own = queries_ref[:, r * half : (r + 1) * half].astype(F32)
        roc[r] = (ALPHA_WEIGHT * own + BETA_WEIGHT * (total / fb_count)).astype(BF16)
    to_outer((4, lambda r, b: roc.at[r], roc_in))

    for r in range(2):
        arrived(r, 4, roc_in)

    @pl.loop(0, across)
    def _(t):
        far_x = (x + turn_of(t)) % across
        there = pl.ds(far_x * ring, ring)
        for r in range(2):
            picked = jnp.dot(
                select[r, there].reshape(chunk, held_queries),
                roc_in[r].reshape(held_queries, half),
                preferred_element_type=F32,
            )
            vec[r, there] = picked.astype(BF16).reshape(ring, slab, half)
        to_chunk(t, far_x, (5, vec, vec_in, lambda r: vec_sem.at[r, x]))

    scale = 3.0 / math.sqrt(width)
    live = tiles_ref[0] * TILE
    bits = slab // 2
    turn = iota((slab, LANES), 0) == iota((slab, LANES), 1) % slab

    def swapped(index):
        o, s, low = index // slab, (index % slab) // bits, index % bits
        return (low // CORES) * slab + s * bits + o * CORES + low % CORES

    swap = jnp.where(
        iota((chunk, chunk), 0) == swapped(iota((chunk, chunk), 1)), 1.0, 0.0
    ).astype(BF16)

    @pl.loop(0, across)
    def _(t):
        far_x = (x + across - turn_of(t)) % across
        there = pl.ds(far_x * ring, ring)
        for r in range(2):
            landed = vec_in.at[r, there]
            pltpu.make_async_copy(landed, landed, vec_sem.at[r, far_x]).wait()
        first = vec_in[0, there].reshape(chunk, half)
        second = jnp.dot(
            swap, vec_in[1, there].reshape(chunk, half), preferred_element_type=F32
        ).astype(BF16)
        scores = lax.dot_general(first, held[:, :half], contract_last, preferred_element_type=F32)
        scores = scores + lax.dot_general(
            second, held[:, half:], contract_last, preferred_element_type=F32
        )
        scores = jnp.where(iota((chunk, rows), 1) < live, scores * scale, NEG_FILL)
        peak = jnp.max(scores, axis=1, keepdims=True)
        weights = jnp.exp(scores - peak)
        mass = jnp.sum(weights, axis=1, keepdims=True)
        value = jnp.dot(weights.astype(BF16), held[...], preferred_element_type=F32)
        value = (value / mass).astype(BF16)
        level = peak + jnp.log(mass)
        part[0, there] = value[:, :half].reshape(ring, slab, half)
        part[1, there] = (
            jnp.dot(swap, value[:, half:], preferred_element_type=F32)
            .astype(BF16)
            .reshape(ring, slab, half)
        )
        sub, lane = iota((chunk, LANES), 0), iota((chunk, LANES), 1) % slab
        for o in range(ring):
            near = level[o * slab : (o + 1) * slab]
            row = jnp.sum(jnp.where(turn, near, 0.0), axis=0, keepdims=True)
            lse[0, far_x * ring + o] = row
            place = swapped(o * slab + lane)
            row = jnp.sum(jnp.where(sub == place, level, 0.0), axis=0, keepdims=True)
            lse[1, far_x * ring + o] = row
        to_chunk(
            t,
            far_x,
            (7, lse, lse_in, lambda r: recv_sem.at[r, 7]),
            (6, part, part_in, lambda r: recv_sem.at[r, 6]),
        )

    square = iota((queries, LANES), 0) == iota((queries, LANES), 1)
    for r in range(2):
        arrived(r, 7, lse_in)
        levels = jnp.concatenate([lane_tile(lse_in, r, j) for j in range(tiles)], axis=1)
        mask = spread[r].astype(F32) > 0.0
        levels = jnp.where(mask, levels, NEG_FILL)
        top = jnp.max(levels, axis=1, keepdims=True)
        weights = jnp.where(mask, jnp.exp(levels - top), 0.0)
        total = jnp.sum(weights, axis=1, keepdims=True)
        high = weights.astype(BF16)
        low = (weights - high.astype(F32)).astype(BF16)
        arrived(r, 6, part_in)
        parts = part_in[r].reshape(slots, half)
        value = jnp.dot(high, parts, preferred_element_type=F32)
        value = value + jnp.dot(low, parts, preferred_element_type=F32)
        some = total > 0.0
        total = jnp.where(some, total, 1.0)
        comb[r] = (value / total).astype(BF16).reshape(blocks, queries, half)
        level = jnp.where(some, top + jnp.log(total), NEG_FILL)
        for b in range(blocks):
            near = level[b * queries : (b + 1) * queries]
            lse2[r, b] = jnp.sum(jnp.where(square, near, 0.0), axis=0, keepdims=True)
    to_outer((9, lambda r, b: lse2.at[r, b], lse2_in), (8, lambda r, b: comb.at[r, b], comb_in))

    for r in range(2):
        arrived(r, 9, lse2_in)
        level = [
            jnp.sum(jnp.where(square, lse2_in[r, b], 0.0), axis=1, keepdims=True)
            for b in range(blocks)
        ]
        top = functools.reduce(jnp.maximum, level)
        factor = [jnp.exp(v - top) for v in level]
        total = functools.reduce(jnp.add, factor)
        arrived(r, 8, comb_in)
        value = jnp.zeros((queries, half), F32)
        for b in range(blocks):
            value = value + factor[b] * comb_in[r, b].astype(F32)
        retrieved_ref[:, r * half : (r + 1) * half] = (value / total).astype(BF16)
        if r == 0:
            log_total = top + jnp.log(total)
            log_row = jnp.sum(jnp.where(square, log_total, 0.0), axis=0, keepdims=True)
            log_ref[...] = log_row[:, :queries]

    for r in range(2):
        for phase, target in (
            (0, table_in),
            (1, asked_in),
            (2, found_in),
            (3, fsum_in),
            (4, roc_in),
            (5, vec_in),
            (6, part_in),
            (7, lse_in),
            (8, comb_in),
            (9, lse2_in),
        ):
            sent(r, phase, target)


def per_device(queries, passages, list_tiles, probes, fb_probe, fb_row):
    groups, members = lax.axis_size("grp"), lax.axis_size("dev")
    rows, width = passages.shape
    query_rows, probe_count = probes.shape
    fb_count = fb_row.shape[1]
    sizes = (groups, members, rows, query_rows, probe_count, fb_count, width)
    lists, half, slab = groups * members, width // 2, SLOTS * groups
    across = members // (groups // CORES)
    slots = members * slab
    tile_lanes = min(LANES, slots)
    vmem = pl.BlockSpec(memory_space=pltpu.VMEM)
    plane_rows = pltpu.VMEM((2, members, slab, half), BF16)
    plane_float = pltpu.VMEM((2, members, 1, LANES), F32)
    outer_rows = pltpu.VMEM((2, groups, query_rows, half), BF16)
    outer_float = pltpu.VMEM((2, groups, 1, LANES), F32)
    retrieved, log_total = pl.pallas_call(
        functools.partial(kernel, sizes),
        out_shape=(
            jax.ShapeDtypeStruct((query_rows, width), BF16),
            jax.ShapeDtypeStruct((1, query_rows), F32),
        ),
        in_specs=[
            vmem,
            vmem,
            vmem,
            vmem,
            pl.BlockSpec(memory_space=pltpu.SMEM),
            pl.BlockSpec(memory_space=pl.ANY),
        ],
        out_specs=(vmem, vmem),
        scratch_shapes=[
            pltpu.VMEM((rows, width), BF16),
            pltpu.VMEM((1, SLOTS * lists), jnp.int32),
            pltpu.VMEM((2, groups, 1, SLOTS * lists), jnp.int32),
            plane_float,
            plane_float,
            pltpu.VMEM((2, members, slab, groups * query_rows), BF16),
            pltpu.VMEM((2, groups * query_rows, slots), BF16),
            plane_rows,
            plane_rows,
            outer_rows,
            outer_rows,
            pltpu.VMEM((2, query_rows, half), BF16),
            outer_rows,
            plane_rows,
            plane_rows,
            plane_rows,
            plane_rows,
            plane_float,
            plane_float,
            outer_rows,
            outer_rows,
            outer_float,
            outer_float,
            pltpu.SemaphoreType.DMA,
            pltpu.SemaphoreType.DMA((2, 10)),
            pltpu.SemaphoreType.DMA((2, 10)),
            pltpu.SemaphoreType.DMA((2, across)),
        ],
        compiler_params=pltpu.CompilerParams(
            collective_id=0, has_side_effects=True, vmem_limit_bytes=56 * 1024 * 1024
        ),
        name="probe_lists",
    )(queries, probes, fb_probe, fb_row, list_tiles, passages)
    return retrieved, log_total.reshape(query_rows)


def solution(mesh):
    spec = P(("grp", "dev"), None)
    flat = P(("grp", "dev"))
    return jax.shard_map(
        per_device,
        mesh=mesh,
        in_specs=(spec, spec, flat, spec, spec, spec),
        out_specs=(spec, flat),
        check_vma=False,
    )
```

time: 149 us -> 133 us (0.89)
  the two profiles are of different devices: /device:TPU:6 before, /device:TPU:4 now
where the time goes in v2:
time: 133 us
  Pallas kernels  129 us (97%)
  local copies, waits for them, and re-layouts  2.52 us (2%)
    pallas_call x1, Pallas kernels, per_device(): pl.pallas_call(functools.partial(kernel, sizes), out_shape=(jax.ShapeDtyp...  129 us

profile of v2, /device:TPU:4, one launch (start us, length us, event | category | flops | bytes accessed | tf_op | source)
XLA Modules:
  0.0 133.0 jit_solution(708229310759102287)
XLA Ops:
  1.3 129.2 %probe_lists.1 = (bf16[16,768]{1,0:T(8,128)(2,1)}, f32[1,16]{1,0:T(1,128)}) custom-call(bf16[16,768]{1,0:T(8,128)(2,1)} %queries_ref.1, s32[16,32]{1,0:T(8,128)} %probes_ref.1, s32[16,10]{1,0:T(8,128)} %fb_probe_ref.1, s32[16,10]{1,0:T(8,128)} %fb_row_ref.1, s32[1]{0:T(128)S(6)} %copy.10.tiles_ref, bf16[2048,768]{1,0:T(8,128)(2,1)} %passages_ref.1), custom_call_target="tpu_custom_call" | custom-call | tf_op jit(solution)/shard_map/probe_lists/pallas_call | solution.py:477
  130.5 1.3 %copy.11 = bf16[16,768]{1,0:T(8,128)(2,1)} copy(bf16[16,768]{1,0:T(8,128)(2,1)} %get-tuple-element.8) | data formatting | bytes 49152
  131.9 1.2 copy.12

commit v3 on v2

--- a/solution.py
+++ b/solution.py
@@ -61,6 +61,7 @@
     send_sem,
     recv_sem,
     vec_sem,
+    vec_sent_sem,
 ):
     groups, members, rows, queries, probe_count, fb_count, width = sizes
     ring = groups // CORES
@@ -80,28 +81,59 @@
     z, c = grp // CORES, grp % CORES
     y, x = dev // across, dev % across
     my_b = (grp, y * CORES + c)
-    my_o = (y, z)
     my_k = (x * ring + y, x * ring + z)
 
-    def outer_id(r, b):
+    def wrap(index, n):
+        return jnp.where(index >= n, index - n, index)
+
+    steps = sorted(range(ring), key=lambda step: -min(step, ring - step))
+    far_y = [wrap(y + step, ring) for step in steps]
+    far_z = [wrap(z + step, ring) for step in steps]
+    dev_y = [v * across for v in far_y]
+    grp_z = [v * CORES for v in far_z]
+    row_y, column_z = y * across, z * CORES
+
+    def plane_place(r, n, far_x):
         if r == 0:
-            return (b, dev)
-        return (z * CORES + b % CORES, (b // CORES) * across + x)
-
-    def plane_id(r, k):
-        far_x, far_o = k // ring, k % ring
+            return far_x * ring + far_y[n], (grp, dev_y[n] + far_x)
+        return far_x * ring + far_z[n], (grp_z[n] + c, row_y + far_x)
+
+    def outer_place(r, n, far_c):
         if r == 0:
-            return (grp, far_o * across + far_x)
-        return (far_o * CORES + c, y * across + far_x)
-
-    def either_way(i, n):
-        return jnp.where(i % 2 == 1, (i + 1) // 2, (n - i // 2) % n)
-
-    def send(r, source, target, phase, landed, place):
+            return grp_z[n] + far_c, (grp_z[n] + far_c, dev)
+        return far_y[n] * CORES + far_c, (column_z + far_c, dev_y[n] + x)
+
+    def far_x_of(t):
+        if across == 4:
+            return jnp.where(t == 0, 0, jnp.where(t == 1, 2, jnp.where(t == 2, 3, 1)))
+        return t
+
+    def each_plane(t, far_x, act):
+        for n in range(ring):
+            for r in range(2):
+                k, place = plane_place(r, n, far_x)
+                if n < ring - 1:
+                    act(r, k, place)
+                else:
+                    pl.when(t > 0)(functools.partial(act, r, k, place))
+
+    def each_outer(act):
+        @pl.loop(0, CORES)
+        def _(t):
+            far_c = jnp.where(t == 0, 1 - c, c)
+            for n in range(ring):
+                for r in range(2):
+                    b, place = outer_place(r, n, far_c)
+                    if n < ring - 1:
+                        act(r, b, place)
+                    else:
+                        pl.when(t < CORES - 1)(functools.partial(act, r, b, place))
+
+    def send(r, source, target, left, landed, place):
         pltpu.make_async_remote_copy(
             src_ref=source,
             dst_ref=target,
-            send_sem=send_sem.at[r, phase],
+            send_sem=left,
             recv_sem=landed,
             device_id=place,
             device_id_type=MESH,
@@ -114,74 +146,52 @@
                     source(r, my_b[r]), target.at[r, my_b[r]], recv_sem.at[r, phase]
                 ).start()
 
-        @pl.loop(0, blocks - 1)
-        def _(i):
-            j = blocks - 1 - i
-            step = either_way(j // CORES, ring)
-            for r in range(2):
-                first = (z, y)[r]
-                b = (first + step) % ring * CORES + (c + j) % CORES
-                for phase, source, target in items:
-                    send(
-                        r,
-                        source(r, b),
-                        target.at[r, my_b[r]],
-                        phase,
-                        recv_sem.at[r, phase],
-                        outer_id(r, b),
-                    )
-
-    def to_plane(phase, source, target):
-        for r in range(2):
-            mine = my_k[r]
-            pltpu.make_async_copy(
-                source.at[r, mine], target.at[r, mine], recv_sem.at[r, phase]
-            ).start()
-
-        @pl.loop(0, plane - 1)
-        def _(i):
-            j = plane - 1 - i
-            step = either_way(j // across, ring)
-            for r in range(2):
-                k = (x + j) % across * ring + (my_o[r] + step) % ring
+        def act(r, b, place):
+            for phase, source, target in items:
                 send(
                     r,
-                    source.at[r, k],
-                    target.at[r, my_k[r]],
-                    phase,
+                    source(r, b),
+                    target.at[r, my_b[r]],
+                    send_sem.at[r, phase],
                     recv_sem.at[r, phase],
-                    plane_id(r, k),
+                    place,
                 )
 
+        each_outer(act)
+
     def to_chunk(t, far_x, *items):
-        @pl.when(t == across - 1)
+        @pl.when(t == 0)
         def _():
             for r in range(2):
-                for phase, source, target, landed in items:
+                for left, source, target, landed in items:
                     pltpu.make_async_copy(
                         source.at[r, my_k[r]], target.at[r, my_k[r]], landed(r)
                     ).start()
 
-        @pl.loop(0, ring)
-        def _(i):
-            step = either_way(ring - 1 - i, ring)
-
-            @pl.when(t + i < across + ring - 2)
-            def _():
-                for r in range(2):
-                    k = far_x * ring + (my_o[r] + step) % ring
-                    for phase, source, target, landed in items:
-                        send(
-                            r,
-                            source.at[r, k],
-                            target.at[r, my_k[r]],
-                            phase,
-                            landed(r),
-                            plane_id(r, k),
-                        )
-
-    def turn_of(t):
-        return (across // 2 + either_way(t, across)) % across
+        def act(r, k, place):
+            for left, source, target, landed in items:
+                send(r, source.at[r, k], target.at[r, my_k[r]], left(r), landed(r), place)
+
+        each_plane(t, far_x, act)
+
+    def both_ends(phase, source, target):
+        return (
+            lambda r: send_sem.at[r, phase],
+            source,
+            target,
+            lambda r: recv_sem.at[r, phase],
+        )
+
+    def chunk_sent(t):
+        for r in range(2):
+            gone = vec.at[r, pl.ds(0, ring - 1 if t == 0 else ring)]
+            pltpu.make_async_copy(gone, gone, vec_sent_sem.at[r, t]).wait()
+
+    def to_plane(phase, source, target):
+        @pl.loop(0, across)
+        def _(t):
+            far_x = wrap(x + far_x_of(t), across)
+            to_chunk(t, far_x, both_ends(phase, source, target))
 
     def arrived(r, phase, target):
         pltpu.make_async_copy(target.at[r], target.at[r], recv_sem.at[r, phase]).wait()
@@ -191,17 +201,15 @@
         pltpu.make_async_copy(gone, gone, send_sem.at[r, phase]).wait()
 
     barrier = pltpu.get_barrier_semaphore()
-    for r in range(2):
-        for partners, mine, place in ((blocks, my_b[r], outer_id), (plane, my_k[r], plane_id)):
-
-            @pl.loop(1, partners)
-            def _(i, r=r, partners=partners, mine=mine, place=place):
-                pl.semaphore_signal(
-                    barrier,
-                    inc=1,
-                    device_id=place(r, (mine + i) % partners),
-                    device_id_type=MESH,
-                )
+
+    def greet(r, index, place):
+        pl.semaphore_signal(barrier, inc=1, device_id=place, device_id_type=MESH)
+
+    each_outer(greet)
+
+    @pl.loop(0, across)
+    def _(t):
+        each_plane(t, wrap(x + far_x_of(t), across), greet)
 
     copy_held = pltpu.make_async_copy(passages_ref, held, held_sem)
     copy_held.start()
@@ -247,8 +255,12 @@
         all_codes = jnp.concatenate(
             [all_codes[:, s * lists : (s + 1) * lists] for s in range(SLOTS)], axis=0
         )
-        far_grp, far_dev = plane_id(r, far_k)
-        list_hot = jnp.where(lane_l == far_grp * members + far_dev, 1.0, 0.0).astype(BF16)
+        far_o, far_column = far_k % ring, far_k // ring
+        if r == 0:
+            far_list = grp * members + far_o * across + far_column
+        else:
+            far_list = (far_o * CORES + c) * members + row_y + far_column
+        list_hot = jnp.where(lane_l == far_list, 1.0, 0.0).astype(BF16)
         want = (all_codes & 255).astype(F32).astype(BF16)
         want_rows = lax.dot_general(
             list_hot,
@@ -333,7 +345,7 @@
 
     @pl.loop(0, across)
     def _(t):
-        far_x = (x + turn_of(t)) % across
+        far_x = wrap(x + far_x_of(t), across)
         there = pl.ds(far_x * ring, ring)
         for r in range(2):
             picked = jnp.dot(
@@ -342,12 +354,19 @@
                 preferred_element_type=F32,
             )
             vec[r, there] = picked.astype(BF16).reshape(ring, slab, half)
-        to_chunk(t, far_x, (5, vec, vec_in, lambda r: vec_sem.at[r, x]))
+        for late in range(2, across):
+            pl.when(t == late)(functools.partial(chunk_sent, late - 2))
+        to_chunk(
+            t,
+            far_x,
+            (lambda r: vec_sent_sem.at[r, t], vec, vec_in, lambda r: vec_sem.at[r, x]),
+        )
 
     scale = 3.0 / math.sqrt(width)
     live = tiles_ref[0] * TILE
     bits = slab // 2
     turn = iota((slab, LANES), 0) == iota((slab, LANES), 1) % slab
+    term_lane = iota((chunk, LANES), 1)
 
     def swapped(index):
         o, s, low = index // slab, (index % slab) // bits, index % bits
@@ -359,7 +378,7 @@
 
     @pl.loop(0, across)
     def _(t):
-        far_x = (x + across - turn_of(t)) % across
+        far_x = wrap(x + wrap(across - far_x_of(t), across), across)
         there = pl.ds(far_x * ring, ring)
         for r in range(2):
             landed = vec_in.at[r, there]
@@ -368,9 +387,11 @@
         second = jnp.dot(
             swap, vec_in[1, there].reshape(chunk, half), preferred_element_type=F32
         ).astype(BF16)
-        scores = lax.dot_general(first, held[:, :half], contract_last, preferred_element_type=F32)
-        scores = scores + lax.dot_general(
-            second, held[:, half:], contract_last, preferred_element_type=F32
+        scores = lax.dot_general(
+            jnp.concatenate([first, second], axis=1),
+            held[...],
+            contract_last,
+            preferred_element_type=F32,
         )
         scores = jnp.where(iota((chunk, rows), 1) < live, scores * scale, NEG_FILL)
         peak = jnp.max(scores, axis=1, keepdims=True)
@@ -380,24 +401,28 @@
         value = (value / mass).astype(BF16)
         level = peak + jnp.log(mass)
         part[0, there] = value[:, :half].reshape(ring, slab, half)
-        part[1, there] = (
-            jnp.dot(swap, value[:, half:], preferred_element_type=F32)
-            .astype(BF16)
-            .reshape(ring, slab, half)
-        )
-        sub, lane = iota((chunk, LANES), 0), iota((chunk, LANES), 1) % slab
+        rest, terms = level, jnp.zeros((chunk, LANES), F32)
+        for i in range(3):
+            term = rest.astype(BF16).astype(F32)
+            terms = jnp.where(term_lane == i, term, terms)
+            rest = rest - term
+        moved = jnp.dot(
+            swap,
+            jnp.concatenate([value[:, half:], terms.astype(BF16)], axis=1),
+            preferred_element_type=F32,
+        )
+        part[1, there] = moved[:, :half].astype(BF16).reshape(ring, slab, half)
+        levels = (level, jnp.sum(moved[:, half:], axis=1, keepdims=True))
         for o in range(ring):
-            near = level[o * slab : (o + 1) * slab]
-            row = jnp.sum(jnp.where(turn, near, 0.0), axis=0, keepdims=True)
-            lse[0, far_x * ring + o] = row
-            place = swapped(o * slab + lane)
-            row = jnp.sum(jnp.where(sub == place, level, 0.0), axis=0, keepdims=True)
-            lse[1, far_x * ring + o] = row
+            for r in range(2):
+                near = levels[r][o * slab : (o + 1) * slab]
+                row = jnp.sum(jnp.where(turn, near, 0.0), axis=0, keepdims=True)
+                lse[r, far_x * ring + o] = row
         to_chunk(
             t,
             far_x,
-            (7, lse, lse_in, lambda r: recv_sem.at[r, 7]),
-            (6, part, part_in, lambda r: recv_sem.at[r, 6]),
+            both_ends(7, lse, lse_in),
+            both_ends(6, part, part_in),
         )
 
     square = iota((queries, LANES), 0) == iota((queries, LANES), 1)
@@ -443,6 +468,8 @@
             log_row = jnp.sum(jnp.where(square, log_total, 0.0), axis=0, keepdims=True)
             log_ref[...] = log_row[:, :queries]
 
+    for t in range(max(0, across - 2), across):
+        chunk_sent(t)
     for r in range(2):
         for phase, target in (
             (0, table_in),
@@ -450,7 +477,6 @@
             (2, found_in),
             (3, fsum_in),
             (4, roc_in),
-            (5, vec_in),
             (6, part_in),
             (7, lse_in),
             (8, comb_in),
@@ -517,6 +543,7 @@
             pltpu.SemaphoreType.DMA((2, 10)),
             pltpu.SemaphoreType.DMA((2, 10)),
             pltpu.SemaphoreType.DMA((2, across)),
+            pltpu.SemaphoreType.DMA((2, across)),
         ],
         compiler_params=pltpu.CompilerParams(
             collective_id=0, has_side_effects=True, vmem_limit_bytes=56 * 1024 * 1024

time: 133 us -> 130 us (0.977)
  the two profiles are of different devices: /device:TPU:4 before, /device:TPU:1 now
where the time goes in v3:
time: 130 us
  Pallas kernels  126 us (97%)
  local copies, waits for them, and re-layouts  2.52 us (2%)
    pallas_call x1, Pallas kernels, per_device(): pl.pallas_call(functools.partial(kernel, sizes), out_shape=(jax.ShapeDtyp...  126 us

profile of v3, /device:TPU:1, one launch (start us, length us, event | category | flops | bytes accessed | tf_op | source)
XLA Modules:
  0.0 130.0 jit_solution(6893007218526929159)
XLA Ops:
  1.3 126.2 %probe_lists.1 = (bf16[16,768]{1,0:T(8,128)(2,1)}, f32[1,16]{1,0:T(1,128)}) custom-call(bf16[16,768]{1,0:T(8,128)(2,1)} %queries_ref.1, s32[16,32]{1,0:T(8,128)} %probes_ref.1, s32[16,10]{1,0:T(8,128)} %fb_probe_ref.1, s32[16,10]{1,0:T(8,128)} %fb_row_ref.1, s32[1]{0:T(128)S(6)} %copy.10.tiles_ref, bf16[2048,768]{1,0:T(8,128)(2,1)} %passages_ref.1), custom_call_target="tpu_custom_call" | custom-call | tf_op jit(solution)/shard_map/probe_lists/pallas_call | solution.py:503
  127.5 1.3 %copy.11 = bf16[16,768]{1,0:T(8,128)(2,1)} copy(bf16[16,768]{1,0:T(8,128)(2,1)} %get-tuple-element.8) | data formatting | bytes 49152
  128.9 1.2 copy.12

commit v4 on v3

--- a/solution.py
+++ b/solution.py
@@ -61,7 +61,6 @@
     send_sem,
     recv_sem,
     vec_sem,
-    vec_sent_sem,
 ):
     groups, members, rows, queries, probe_count, fb_count, width = sizes
     ring = groups // CORES
@@ -181,11 +180,6 @@
             target,
             lambda r: recv_sem.at[r, phase],
         )
-
-    def chunk_sent(t):
-        for r in range(2):
-            gone = vec.at[r, pl.ds(0, ring - 1 if t == 0 else ring)]
-            pltpu.make_async_copy(gone, gone, vec_sent_sem.at[r, t]).wait()
 
     def to_plane(phase, source, target):
         @pl.loop(0, across)
@@ -354,12 +348,10 @@
                 preferred_element_type=F32,
             )
             vec[r, there] = picked.astype(BF16).reshape(ring, slab, half)
-        for late in range(2, across):
-            pl.when(t == late)(functools.partial(chunk_sent, late - 2))
         to_chunk(
             t,
             far_x,
-            (lambda r: vec_sent_sem.at[r, t], vec, vec_in, lambda r: vec_sem.at[r, x]),
+            (lambda r: send_sem.at[r, 5], vec, vec_in, lambda r: vec_sem.at[r, x]),
         )
 
     scale = 3.0 / math.sqrt(width)
@@ -468,8 +460,6 @@
             log_row = jnp.sum(jnp.where(square, log_total, 0.0), axis=0, keepdims=True)
             log_ref[...] = log_row[:, :queries]
 
-    for t in range(max(0, across - 2), across):
-        chunk_sent(t)
     for r in range(2):
         for phase, target in (
             (0, table_in),
@@ -477,6 +467,7 @@
             (2, found_in),
             (3, fsum_in),
             (4, roc_in),
+            (5, vec_in),
             (6, part_in),
             (7, lse_in),
             (8, comb_in),
@@ -543,7 +534,6 @@
             pltpu.SemaphoreType.DMA((2, 10)),
             pltpu.SemaphoreType.DMA((2, 10)),
             pltpu.SemaphoreType.DMA((2, across)),
-            pltpu.SemaphoreType.DMA((2, across)),
         ],
         compiler_params=pltpu.CompilerParams(
             collective_id=0, has_side_effects=True, vmem_limit_bytes=56 * 1024 * 1024

time: 130 us -> 126 us (0.969)
  the two profiles are of different devices: /device:TPU:1 before, /device:TPU:6 now
where the time goes in v4:
time: 126 us; the launch traced here: 125 us
  Pallas kernels  122 us (97%)
  local copies, waits for them, and re-layouts  2.52 us (2%)
  between operations  1.28 us (1%)
    pallas_call x1, Pallas kernels, per_device(): pl.pallas_call(functools.partial(kernel, sizes), out_shape=(jax.ShapeDtyp...  122 us
    unnamed x2, local copies, waits for them, and re-layouts  2.52 us

profile of v4, /device:TPU:6, one launch (start us, length us, event | category | flops | bytes accessed | tf_op | source)
XLA Modules:
  0.0 125.4 jit_solution(12907814009508516064)
XLA Ops:
  1.3 121.6 %probe_lists.1 = (bf16[16,768]{1,0:T(8,128)(2,1)}, f32[1,16]{1,0:T(1,128)}) custom-call(bf16[16,768]{1,0:T(8,128)(2,1)} %queries_ref.1, s32[16,32]{1,0:T(8,128)} %probes_ref.1, s32[16,10]{1,0:T(8,128)} %fb_probe_ref.1, s32[16,10]{1,0:T(8,128)} %fb_row_ref.1, s32[1]{0:T(128)S(6)} %copy.10.tiles_ref, bf16[2048,768]{1,0:T(8,128)(2,1)} %passages_ref.1), custom_call_target="tpu_custom_call" | custom-call | tf_op jit(solution)/shard_map/probe_lists/pallas_call | solution.py:494
  122.8 1.3 %copy.11 = bf16[16,768]{1,0:T(8,128)(2,1)} copy(bf16[16,768]{1,0:T(8,128)(2,1)} %get-tuple-element.8) | data formatting | bytes 49152
  124.2 1.2 copy.12

commit v5 on v4

--- a/solution.py
+++ b/solution.py
@@ -116,12 +116,12 @@
                 else:
                     pl.when(t > 0)(functools.partial(act, r, k, place))
 
-    def each_outer(act):
+    def each_outer(act, routes=(0, 1)):
         @pl.loop(0, CORES)
         def _(t):
             far_c = jnp.where(t == 0, 1 - c, c)
             for n in range(ring):
-                for r in range(2):
+                for r in routes:
                     b, place = outer_place(r, n, far_c)
                     if n < ring - 1:
                         act(r, b, place)
@@ -138,8 +138,8 @@
             device_id_type=MESH,
         ).start()
 
-    def to_outer(*items):
-        for r in range(2):
+    def to_outer(*items, routes=(0, 1)):
+        for r in routes:
             for phase, source, target in items:
                 pltpu.make_async_copy(
                     source(r, my_b[r]), target.at[r, my_b[r]], recv_sem.at[r, phase]
@@ -156,7 +156,7 @@
                     place,
                 )
 
-        each_outer(act)
+        each_outer(act, routes)
 
     def to_chunk(t, far_x, *items):
         @pl.when(t == 0)
@@ -323,7 +323,7 @@
         arrived(r, 2, found_in)
         total = jnp.dot(spread[r], found_in[r].reshape(slots, half), preferred_element_type=F32)
         fsum[r] = total.astype(BF16).reshape(blocks, queries, half)
-    to_outer((3, lambda r, b: fsum.at[r, b], fsum_in))
+        to_outer((3, lambda r, b: fsum.at[r, b], fsum_in), routes=(r,))
 
     for r in range(2):
         arrived(r, 3, fsum_in)
@@ -332,7 +332,7 @@
             total = total + fsum_in[r, b].astype(F32)
         own = queries_ref[:, r * half : (r + 1) * half].astype(F32)
         roc[r] = (ALPHA_WEIGHT * own + BETA_WEIGHT * (total / fb_count)).astype(BF16)
-    to_outer((4, lambda r, b: roc.at[r], roc_in))
+        to_outer((4, lambda r, b: roc.at[r], roc_in), routes=(r,))
 
     for r in range(2):
         arrived(r, 4, roc_in)
@@ -439,7 +439,11 @@
         for b in range(blocks):
             near = level[b * queries : (b + 1) * queries]
             lse2[r, b] = jnp.sum(jnp.where(square, near, 0.0), axis=0, keepdims=True)
-    to_outer((9, lambda r, b: lse2.at[r, b], lse2_in), (8, lambda r, b: comb.at[r, b], comb_in))
+        to_outer(
+            (9, lambda r, b: lse2.at[r, b], lse2_in),
+            (8, lambda r, b: comb.at[r, b], comb_in),
+            routes=(r,),
+        )
 
     for r in range(2):
         arrived(r, 9, lse2_in)

time: 126 us -> 123 us (0.976)
  Pallas kernels: 122 us -> 119 us
    pallas_call x1, Pallas kernels: 122 us -> 119 us  [per_device(): pl.pallas_call(functools.partial(kernel, sizes), out_shape=(jax.ShapeDtyp...]
where the time goes in v5:
time: 123 us
  Pallas kernels  119 us (97%)
  local copies, waits for them, and re-layouts  2.52 us (2%)
  between operations  1.28 us (1%)
    pallas_call x1, Pallas kernels, per_device(): pl.pallas_call(functools.partial(kernel, sizes), out_shape=(jax.ShapeDtyp...  119 us
    unnamed x2, local copies, waits for them, and re-layouts  2.52 us

profile of v5, /device:TPU:6, one launch (start us, length us, event | category | flops | bytes accessed | tf_op | source)
XLA Modules:
  0.0 122.9 jit_solution(16410272109691800480)
XLA Ops:
  1.3 119.1 %probe_lists.1 = (bf16[16,768]{1,0:T(8,128)(2,1)}, f32[1,16]{1,0:T(1,128)}) custom-call(bf16[16,768]{1,0:T(8,128)(2,1)} %queries_ref.1, s32[16,32]{1,0:T(8,128)} %probes_ref.1, s32[16,10]{1,0:T(8,128)} %fb_probe_ref.1, s32[16,10]{1,0:T(8,128)} %fb_row_ref.1, s32[1]{0:T(128)S(6)} %copy.10.tiles_ref, bf16[2048,768]{1,0:T(8,128)(2,1)} %passages_ref.1), custom_call_target="tpu_custom_call" | custom-call | tf_op jit(solution)/shard_map/probe_lists/pallas_call | solution.py:498
  120.4 1.3 %copy.11 = bf16[16,768]{1,0:T(8,128)(2,1)} copy(bf16[16,768]{1,0:T(8,128)(2,1)} %get-tuple-element.8) | data formatting | bytes 49152
  121.7 1.2 copy.12
